TPU v7x, 32 devices: a whole 2x2x4 slice. The times are simulated.
32 devices in a mesh: groups: 2 (over y), sub: 4 (over z), blk: 4 (over x, core).
Axes of the slice: x: 2, y: 2, z: 4, core: 2. Of those that a mesh axis runs over, the one named last changes fastest.
Arguments:
- conductance: float32 [128, 8192], P(('groups', 'sub'), 'blk'), parts along dimension 0, may hold values from 0.1 to 10
- source_mask: int32 [128, 8192], P(('groups', 'sub'), 'blk'), parts along dimension 0, may hold values 0 or 1
- ground_mask: int32 [128, 8192], P(('groups', 'sub'), 'blk'), parts along dimension 0, may hold values 0 or 1
- nodata_mask: int32 [128, 8192], P(('groups', 'sub'), 'blk'), parts along dimension 0, may hold values 0 or 1
Outputs:
- potential: float32 [128, 8192], P(('groups', 'sub'), 'blk'), parts along dimension 0
There are 2 independent parts, one for each index of `groups`. A program takes and returns all parts, laid end to end along the dimension named above; each array names one. Nothing has to cross between parts.
All inputs are finite; a program needn't handle non-finite values. No bound on the sum of `source_mask` or of `ground_mask` or of `nodata_mask` on one device may be relied on, other than what follows from the above.
Results may differ from a plain program's by a relative error of at most 0.0003.
Values sent between devices are 32-bit elements; how exact they have to be, the bound alone decides.
A program may use at most 64 MiB of HBM per device.

v0:
```python
import jax
import jax.numpy as jnp
from jax import lax
from jax.sharding import PartitionSpec as P

LEVELS = 5
PRE_SWEEPS = 2
POST_SWEEPS = 2


smooth_low = 0.5
smooth_high = 2.0
coarse_low = 0.02
coarse_high = 2.0
shifts_list = ((1, 0), (-1, 0), (0, 1), (0, -1))


def extended(shard, sides, width):
    for axis, dim in sides:
        size, length = (lax.axis_size(axis), shard.shape[dim])
        up = [(i, (i + 1) % size) for i in range(size - 1)]
        down = [(j, i) for i, j in up]
        last = lax.slice_in_dim(shard, length - width, length, axis=dim)
        leading = lax.slice_in_dim(shard, 0, width, axis=dim)
        before = lax.ppermute(last, axis, up)
        after = lax.ppermute(leading, axis, down)
        shard = jnp.concatenate([before, shard, after], axis=dim)
    return shard


def chebyshev_terms(sweep_count, low_end, high_end):
    mid_point = 0.5 * (high_end + low_end)
    half_width = 0.5 * (high_end - low_end)
    sigma_value = mid_point / half_width
    rho_value = 1.0 / sigma_value
    coefficients = [(0.0, 1.0 / mid_point)]
    for step_index in range(1, sweep_count):
        rho_next = 1.0 / (2.0 * sigma_value - rho_value)
        coefficients.append((rho_next * rho_value, 2.0 * rho_next / half_width))
        rho_value = rho_next
    return coefficients


def pad_zero(field):
    return jnp.pad(field, 1)


def neighbor_of(padded, row_shift, col_shift):
    row_total = padded.shape[0]
    col_total = padded.shape[1]
    return padded[
        1 + row_shift : row_total - 1 + row_shift, 1 + col_shift : col_total - 1 + col_shift
    ]


def level_operator(cond_level, ground_admit, padded_cond):
    validity = jnp.where(cond_level > 0.0, 1.0, 0.0).astype(jnp.float32)
    padded_valid = jnp.where(padded_cond > 0.0, 1.0, 0.0).astype(jnp.float32)
    edges = []
    for row_shift, col_shift in shifts_list:
        other_cond = neighbor_of(padded_cond, row_shift, col_shift)
        other_valid = neighbor_of(padded_valid, row_shift, col_shift)
        edges.append(validity * other_valid * 0.5 * (cond_level + other_cond))
    diagonal = edges[0] + edges[1] + edges[2] + edges[3] + ground_admit + (1.0 - validity)
    precond = jnp.maximum(diagonal, 0.25 * cond_level)
    return (tuple(edges), diagonal, precond, validity)


def apply_operator(operator, padded_field, field):
    result = operator[1] * field
    for edge_index in range(4):
        row_shift, col_shift = shifts_list[edge_index]
        result = result - operator[0][edge_index] * neighbor_of(padded_field, row_shift, col_shift)
    return result


def smooth(operator, padder, source_term, iterate, coefficients):
    update = None
    for keep_part, fresh_part in coefficients:
        if iterate is None:
            residual = source_term
            iterate = jnp.zeros_like(source_term)
        else:
            residual = source_term - apply_operator(operator, padder(iterate), iterate)
        scaled = residual / operator[2]
        if update is None:
            update = fresh_part * scaled
        else:
            update = keep_part * update + fresh_part * scaled
        iterate = iterate + update
    return iterate


def coarsen_sum(field):
    return field.reshape(field.shape[0] // 2, 2, field.shape[1] // 2, 2).sum(axis=(1, 3))


def prolong(field):
    return jnp.repeat(jnp.repeat(field, 2, axis=0), 2, axis=1)


def level_rims(cond_level):
    return extended(cond_level, (("sub", 0), ("blk", 1)), 1)


def face_rims(field):
    return extended(field, (("sub", 0), ("blk", 1)), 1)


def assemble(stacked, sub_count, blk_count):
    member_count = stacked.shape[1]
    row_len = stacked.shape[2]
    col_len = stacked.shape[3]
    shaped = stacked.reshape(sub_count, blk_count, member_count, row_len, col_len)
    shaped = shaped.transpose(2, 0, 3, 1, 4)
    return shaped.reshape(member_count, sub_count * row_len, blk_count * col_len)


def body(conductance, source_mask, ground_mask, nodata_mask):
    validity = 1.0 - nodata_mask.astype(jnp.float32)
    cond_level = conductance * validity
    ground_admit = ground_mask.astype(jnp.float32) * cond_level
    right_side = validity * (source_mask.astype(jnp.float32) - 0.125)
    pre_terms = chebyshev_terms(PRE_SWEEPS, smooth_low, smooth_high)
    post_terms = chebyshev_terms(POST_SWEEPS, smooth_low, smooth_high)
    stored = []
    for level_index in range(LEVELS - 1):
        operator = level_operator(cond_level, ground_admit, level_rims(cond_level))
        iterate = smooth(operator, face_rims, right_side, None, pre_terms)
        residual = right_side - apply_operator(operator, face_rims(iterate), iterate)
        stored.append((operator, right_side, iterate))
        right_side = coarsen_sum(residual)
        cond_level = 0.25 * coarsen_sum(cond_level)
        ground_admit = coarsen_sum(ground_admit)
    row_len = right_side.shape[0]
    col_len = right_side.shape[1]
    coarse_count = 8 + row_len * lax.axis_size("sub") // 2
    coarse_terms = chebyshev_terms(coarse_count, coarse_low, coarse_high)
    sub_count = lax.axis_size("sub")
    blk_count = lax.axis_size("blk")
    paired = jnp.stack([cond_level, ground_admit])[None]
    coef_all = lax.all_gather(paired, ("sub", "blk"), axis=0, tiled=True)
    resid_all = lax.all_gather(right_side[None, None], ("sub", "blk"), axis=0, tiled=True)
    coef_grid = assemble(coef_all, sub_count, blk_count)
    resid_grid = assemble(resid_all, sub_count, blk_count)[0]
    operator = level_operator(coef_grid[0], coef_grid[1], pad_zero(coef_grid[0]))
    whole_grid = smooth(operator, pad_zero, resid_grid, None, coarse_terms)
    row_start = lax.axis_index("sub") * row_len
    col_start = lax.axis_index("blk") * col_len
    iterate = lax.dynamic_slice(whole_grid, (row_start, col_start), (row_len, col_len))
    for level_index in reversed(range(LEVELS - 1)):
        operator, right_side, previous = stored[level_index]
        iterate = previous + operator[3] * prolong(iterate)
        iterate = smooth(operator, face_rims, right_side, iterate, post_terms)
    return iterate


def solution(mesh):
    placed = (
        P(("groups", "sub"), "blk"),
        P(("groups", "sub"), "blk"),
        P(("groups", "sub"), "blk"),
        P(("groups", "sub"), "blk"),
    )
    return jax.shard_map(
        body, mesh=mesh, in_specs=placed, out_specs=P(("groups", "sub"), "blk"), check_vma=False
    )
```

profile of v0, /device:TPU:0, one launch (start us, length us, event | category | flops | bytes accessed | tf_op | source)
XLA Modules:
  0.0 383.2 jit_solution(18202001283506541310)
XLA Ops:
  2.4 5.6 %collective-permute-start = (f32[1,2048]{1,0:T(1,128)S(1)}, f32[1,2048]{1,0:T(1,128)S(1)}, u32[]{:S(2)}, u32[]{:S(2)}) collective-permute-start(f32[1,2048]{1,0:T(1,128)S(1)} %get-tuple-element.76), channel_id=1, source_target_pairs={{0,4},{4,8},{8,12},{1,5},{5,9},{9,13},{2,6},{6,10},{10,14},{3,7},{... | collective-permute-start | bytes 24584 | tf_op jit(solution)/shard_map/ppermute | solution.py:25
  8.0 10.6 %reshape.87 = f32[8,2,1024,2]{3,2,1,0:T(8,128)} reshape(f32[16,2048]{1,0:T(8,128)S(1)} %get-tuple-element.33) | data formatting | bytes 262144 | tf_op jit(solution)/shard_map/reshape | solution.py:95
  18.5 4.5 %reduce_sum.124 = f32[8,1024]{1,0:T(8,128)S(1)} reduce(f32[8,2,1024,2]{3,2,1,0:T(8,128)} %reshape.87, f32[]{:T(128)} %constant.36.clone.1), dimensions={1,3}, to_apply=%region_1.2 | reduce | flops 24576 | bytes 163844 | tf_op jit(solution)/shard_map/reduce_sum | solution.py:95
  28.8 5.2 %collective-permute-start.36 = (f32[1,256]{1,0:T(1,128)S(1)}, f32[1,256]{1,0:T(1,128)S(1)}, u32[]{:S(2)}, u32[]{:S(2)}) collective-permute-start(f32[1,256]{1,0:T(1,128)S(1)} %get-tuple-element.142), channel_id=1, source_target_pairs={{0,4},{4,8},{8,12},{1,5},{5,9},{9,13},{2,6},{6,10},{10,14},{3,7},{... | collective-permute-start | bytes 3080 | tf_op jit(solution)/shard_map/ppermute | solution.py:25
  35.9 20.5 %all-gather.1 = f32[32,1,128]{2,1,0:T(1,128)S(1)} all-gather(f32[2,1,128]{2,1,0:T(1,128)S(1)} %pad_maximum_fusion.206), channel_id=3, replica_groups=mesh['groups'=2,'sub'=4,'blk'=4] {'sub','blk'}, dimensions={0}, use_global_device_ids=true | all-gather | bytes 17408 | tf_op jit(solution)/shard_map/all_gather | solution.py:142
  57.1 10.6 %reshape.88 = f32[8,2,1024,2]{3,2,1,0:T(8,128)} reshape(f32[16,2048]{1,0:T(8,128)S(1)} %get-tuple-element.32) | data formatting | bytes 262144 | tf_op jit(solution)/shard_map/reshape | solution.py:95
  67.6 4.6 %reduce_sum.125 = f32[8,1024]{1,0:T(8,128)S(1)} reduce(f32[8,2,1024,2]{3,2,1,0:T(8,128)} %reshape.88, f32[]{:T(128)} %constant.36.clone.1), dimensions={1,3}, to_apply=%region_2.3 | reduce | flops 24576 | bytes 163844 | tf_op jit(solution)/shard_map/reduce_sum | solution.py:95
  79.1 4.5 %collective-permute-start.24 = (f32[1,512]{1,0:T(1,128)S(1)}, f32[1,512]{1,0:T(1,128)S(1)}, u32[]{:S(2)}, u32[]{:S(2)}) collective-permute-start(f32[1,512]{1,0:T(1,128)S(1)} %get-tuple-element.120), channel_id=1, source_target_pairs={{0,4},{4,8},{8,12},{1,5},{5,9},{9,13},{2,6},{6,10},{10,14},{3,7},{... | collective-permute-start | bytes 6152 | tf_op jit(solution)/shard_map/ppermute | solution.py:25
  85.1 3.0 collective-permute-start.2
  97.3 5.1 %collective-permute-start.14 = (f32[10,1]{1,0:T(8,128)S(1)}, f32[10,1]{1,0:T(8,128)S(1)}, u32[]{:S(2)}, u32[]{:S(2)}) collective-permute-start(f32[10,1]{1,0:T(8,128)S(1)} %get-tuple-element.78), channel_id=1, source_target_pairs={{0,1},{1,2},{2,3},{4,5},{5,6},{6,7},{8,9},{9,10},{10,11},{12,13},{... | collective-permute-start | bytes 128 | tf_op jit(solution)/shard_map/ppermute | solution.py:25
  104.7 3.0 collective-permute-start.7
  108.8 4.5 %collective-permute-start.9 = (f32[1,2048]{1,0:T(1,128)S(1)}, f32[1,2048]{1,0:T(1,128)S(1)}, u32[]{:S(2)}, u32[]{:S(2)}) collective-permute-start(f32[1,2048]{1,0:T(1,128)S(1)} %get-tuple-element.71), channel_id=1, source_target_pairs={{0,4},{4,8},{8,12},{1,5},{5,9},{9,13},{2,6},{6,10},{10,14},{3,7},{... | collective-permute-start | bytes 24584 | tf_op jit(solution)/shard_map/ppermute | solution.py:25
  114.7 4.2 %collective-permute-done.8 = f32[1,2048]{1,0:T(1,128)S(1)} collective-permute-done((f32[1,2048]{1,0:T(1,128)S(1)}, f32[1,2048]{1,0:T(1,128)S(1)}, u32[]{:S(2)}, u32[]{:S(2)}) %collective-permute-start.8) | collective-permute-done | bytes 8224 | tf_op jit(solution)/shard_map/ppermute | solution.py:26
  120.2 3.0 collective-permute-start.11
  124.3 10.6 %reshape.86 = f32[8,2,1024,2]{3,2,1,0:T(8,128)} reshape(f32[16,2048]{1,0:T(8,128)S(1)} %fusion.35) | data formatting | bytes 262144 | tf_op jit(solution)/shard_map/reshape | solution.py:95
  134.8 4.5 %reduce_sum.123 = f32[8,1024]{1,0:T(8,128)S(1)} reduce(f32[8,2,1024,2]{3,2,1,0:T(8,128)} %reshape.86, f32[]{:T(128)} %constant.36.clone.1), dimensions={1,3}, to_apply=%region_0.1 | reduce | flops 24576 | bytes 163844 | tf_op jit(solution)/shard_map/reduce_sum | solution.py:95
  143.1 5.2 %collective-permute-start.26 = (f32[6,1]{1,0:T(8,128)S(1)}, f32[6,1]{1,0:T(8,128)S(1)}, u32[]{:S(2)}, u32[]{:S(2)}) collective-permute-start(f32[6,1]{1,0:T(8,128)S(1)} %get-tuple-element.107), channel_id=1, source_target_pairs={{0,1},{1,2},{2,3},{4,5},{5,6},{6,7},{8,9},{9,10},{10,11},{12,13},{... | collective-permute-start | bytes 80 | tf_op jit(solution)/shard_map/ppermute | solution.py:25
  151.0 5.7 %collective-permute-start.19 = (f32[10,1]{1,0:T(8,128)S(1)}, f32[10,1]{1,0:T(8,128)S(1)}, u32[]{:S(2)}, u32[]{:S(2)}) collective-permute-start(f32[10,1]{1,0:T(8,128)S(1)} %get-tuple-element.86), channel_id=1, source_target_pairs={{0,1},{1,2},{2,3},{4,5},{5,6},{6,7},{8,9},{9,10},{10,11},{12,13},{... | collective-permute-start | bytes 128 | tf_op jit(solution)/shard_map/ppermute | solution.py:25
  157.7 4.5 %collective-permute-start.21 = (f32[1,1024]{1,0:T(1,128)S(1)}, f32[1,1024]{1,0:T(1,128)S(1)}, u32[]{:S(2)}, u32[]{:S(2)}) collective-permute-start(f32[1,1024]{1,0:T(1,128)S(1)} %get-tuple-element.91), channel_id=1, source_target_pairs={{0,4},{4,8},{8,12},{1,5},{5,9},{9,13},{2,6},{6,10},{10,14},{3,7},{... | collective-permute-start | bytes 12296 | tf_op jit(solution)/shard_map/ppermute | solution.py:25
  163.7 4.1 %collective-permute-done.20 = f32[1,1024]{1,0:T(1,128)S(1)} collective-permute-done((f32[1,1024]{1,0:T(1,128)S(1)}, f32[1,1024]{1,0:T(1,128)S(1)}, u32[]{:S(2)}, u32[]{:S(2)}) %collective-permute-start.20) | collective-permute-done | bytes 4128 | tf_op jit(solution)/shard_map/ppermute | solution.py:26
  169.1 3.0 collective-permute-start.23
  180.5 5.0 %collective-permute-start.38 = (f32[4,1]{1,0:T(4,128)S(1)}, f32[4,1]{1,0:T(4,128)S(1)}, u32[]{:S(2)}, u32[]{:S(2)}) collective-permute-start(f32[4,1]{1,0:T(4,128)S(1)} %get-tuple-element.129), channel_id=1, source_target_pairs={{0,1},{1,2},{2,3},{4,5},{5,6},{6,7},{8,9},{9,10},{10,11},{12,13},{... | collective-permute-start | bytes 56 | tf_op jit(solution)/shard_map/ppermute | solution.py:25
  188.2 5.7 %collective-permute-start.31 = (f32[6,1]{1,0:T(8,128)S(1)}, f32[6,1]{1,0:T(8,128)S(1)}, u32[]{:S(2)}, u32[]{:S(2)}) collective-permute-start(f32[6,1]{1,0:T(8,128)S(1)} %get-tuple-element.106), channel_id=1, source_target_pairs={{0,1},{1,2},{2,3},{4,5},{5,6},{6,7},{8,9},{9,10},{10,11},{12,13},{... | collective-permute-start | bytes 80 | tf_op jit(solution)/shard_map/ppermute | solution.py:25
  194.9 4.5 %collective-permute-start.33 = (f32[1,512]{1,0:T(1,128)S(1)}, f32[1,512]{1,0:T(1,128)S(1)}, u32[]{:S(2)}, u32[]{:S(2)}) collective-permute-start(f32[1,512]{1,0:T(1,128)S(1)} %get-tuple-element.115), channel_id=1, source_target_pairs={{0,4},{4,8},{8,12},{1,5},{5,9},{9,13},{2,6},{6,10},{10,14},{3,7},{... | collective-permute-start | bytes 6152 | tf_op jit(solution)/shard_map/ppermute | solution.py:25
  201.5 3.4 collective-permute-done.32
  206.3 3.0 collective-permute-start.35
  216.1 3.2 collective-permute-done.40
  220.6 4.5 %collective-permute-start.43 = (f32[4,1]{1,0:T(4,128)S(1)}, f32[4,1]{1,0:T(4,128)S(1)}, u32[]{:S(2)}, u32[]{:S(2)}) collective-permute-start(f32[4,1]{1,0:T(4,128)S(1)} %get-tuple-element.128), channel_id=1, source_target_pairs={{0,1},{1,2},{2,3},{4,5},{5,6},{6,7},{8,9},{9,10},{10,11},{12,13},{... | collective-permute-start | bytes 56 | tf_op jit(solution)/shard_map/ppermute | solution.py:25
  230.3 4.1 %collective-permute-done.44 = f32[1,256]{1,0:T(1,128)S(1)} collective-permute-done((f32[1,256]{1,0:T(1,128)S(1)}, f32[1,256]{1,0:T(1,128)S(1)}, u32[]{:S(2)}, u32[]{:S(2)}) %collective-permute-start.44) | collective-permute-done | bytes 1056 | tf_op jit(solution)/shard_map/ppermute | solution.py:26
  235.8 4.4 %collective-permute-start.47 = (f32[4,1]{1,0:T(4,128)S(1)}, f32[4,1]{1,0:T(4,128)S(1)}, u32[]{:S(2)}, u32[]{:S(2)}) collective-permute-start(f32[4,1]{1,0:T(4,128)S(1)} %get-tuple-element.126), channel_id=1, source_target_pairs={{0,1},{1,2},{2,3},{4,5},{5,6},{6,7},{8,9},{9,10},{10,11},{12,13},{... | collective-permute-start | bytes 56 | tf_op jit(solution)/shard_map/ppermute | solution.py:25
  242.0 22.8 %all-gather.2 = f32[16,1,128]{2,1,0:T(1,128)S(1)} all-gather(f32[1,1,128]{2,1,0:T(1,128)S(1)} %bitcast.67), channel_id=2, replica_groups=mesh['groups'=2,'sub'=4,'blk'=4] {'sub','blk'}, dimensions={0}, use_global_device_ids=true | all-gather | bytes 8704 | tf_op jit(solution)/shard_map/all_gather | solution.py:143
  270.4 4.2 %collective-permute-done.48 = f32[1,256]{1,0:T(1,128)S(1)} collective-permute-done((f32[1,256]{1,0:T(1,128)S(1)}, f32[1,256]{1,0:T(1,128)S(1)}, u32[]{:S(2)}, u32[]{:S(2)}) %collective-permute-start.48) | collective-permute-done | bytes 1056 | tf_op jit(solution)/shard_map/ppermute | solution.py:26
  276.0 3.0 collective-permute-start.51
  283.6 4.2 %collective-permute-done.52 = f32[1,256]{1,0:T(1,128)S(1)} collective-permute-done((f32[1,256]{1,0:T(1,128)S(1)}, f32[1,256]{1,0:T(1,128)S(1)}, u32[]{:S(2)}, u32[]{:S(2)}) %collective-permute-start.52) | collective-permute-done | bytes 1056 | tf_op jit(solution)/shard_map/ppermute | solution.py:26
  289.1 3.0 collective-permute-start.55
  294.1 2.7 collective-permute-start.57
  298.1 4.2 %collective-permute-done.56 = f32[1,512]{1,0:T(1,128)S(1)} collective-permute-done((f32[1,512]{1,0:T(1,128)S(1)}, f32[1,512]{1,0:T(1,128)S(1)}, u32[]{:S(2)}, u32[]{:S(2)}) %collective-permute-start.56) | collective-permute-done | bytes 2080 | tf_op jit(solution)/shard_map/ppermute | solution.py:26
  303.6 3.5 collective-permute-start.59
  311.6 4.2 %collective-permute-done.60 = f32[1,512]{1,0:T(1,128)S(1)} collective-permute-done((f32[1,512]{1,0:T(1,128)S(1)}, f32[1,512]{1,0:T(1,128)S(1)}, u32[]{:S(2)}, u32[]{:S(2)}) %collective-permute-start.60) | collective-permute-done | bytes 2080 | tf_op jit(solution)/shard_map/ppermute | solution.py:26
  317.1 4.5 %collective-permute-start.63 = (f32[6,1]{1,0:T(8,128)S(1)}, f32[6,1]{1,0:T(8,128)S(1)}, u32[]{:S(2)}, u32[]{:S(2)}) collective-permute-start(f32[6,1]{1,0:T(8,128)S(1)} %get-tuple-element.100), channel_id=1, source_target_pairs={{0,1},{1,2},{2,3},{4,5},{5,6},{6,7},{8,9},{9,10},{10,11},{12,13},{... | collective-permute-start | bytes 80 | tf_op jit(solution)/shard_map/ppermute | solution.py:25
  326.6 4.2 %collective-permute-done.64 = f32[1,1024]{1,0:T(1,128)S(1)} collective-permute-done((f32[1,1024]{1,0:T(1,128)S(1)}, f32[1,1024]{1,0:T(1,128)S(1)}, u32[]{:S(2)}, u32[]{:S(2)}) %collective-permute-start.64) | collective-permute-done | bytes 4128 | tf_op jit(solution)/shard_map/ppermute | solution.py:26
  332.2 4.5 %collective-permute-start.67 = (f32[10,1]{1,0:T(8,128)S(1)}, f32[10,1]{1,0:T(8,128)S(1)}, u32[]{:S(2)}, u32[]{:S(2)}) collective-permute-start(f32[10,1]{1,0:T(8,128)S(1)} %get-tuple-element.82), channel_id=1, source_target_pairs={{0,1},{1,2},{2,3},{4,5},{5,6},{6,7},{8,9},{9,10},{10,11},{12,13},{... | collective-permute-start | bytes 128 | tf_op jit(solution)/shard_map/ppermute | solution.py:25
  341.1 4.2 %collective-permute-done.68 = f32[1,1024]{1,0:T(1,128)S(1)} collective-permute-done((f32[1,1024]{1,0:T(1,128)S(1)}, f32[1,1024]{1,0:T(1,128)S(1)}, u32[]{:S(2)}, u32[]{:S(2)}) %collective-permute-start.68) | collective-permute-done | bytes 4128 | tf_op jit(solution)/shard_map/ppermute | solution.py:26
  346.6 4.5 %collective-permute-start.71 = (f32[10,1]{1,0:T(8,128)S(1)}, f32[10,1]{1,0:T(8,128)S(1)}, u32[]{:S(2)}, u32[]{:S(2)}) collective-permute-start(f32[10,1]{1,0:T(8,128)S(1)} %get-tuple-element.80), channel_id=1, source_target_pairs={{0,1},{1,2},{2,3},{4,5},{5,6},{6,7},{8,9},{9,10},{10,11},{12,13},{... | collective-permute-start | bytes 128 | tf_op jit(solution)/shard_map/ppermute | solution.py:25
  356.7 4.2 %collective-permute-done.72 = f32[1,2048]{1,0:T(1,128)S(1)} collective-permute-done((f32[1,2048]{1,0:T(1,128)S(1)}, f32[1,2048]{1,0:T(1,128)S(1)}, u32[]{:S(2)}, u32[]{:S(2)}) %collective-permute-start.72) | collective-permute-done | bytes 8224 | tf_op jit(solution)/shard_map/ppermute | solution.py:26
  362.2 4.5 %collective-permute-start.75 = (f32[18,1]{1,0:T(8,128)S(1)}, f32[18,1]{1,0:T(8,128)S(1)}, u32[]{:S(2)}, u32[]{:S(2)}) collective-permute-start(f32[18,1]{1,0:T(8,128)S(1)} %get-tuple-element.62), channel_id=1, source_target_pairs={{0,1},{1,2},{2,3},{4,5},{5,6},{6,7},{8,9},{9,10},{10,11},{12,13},{... | collective-permute-start | bytes 224 | tf_op jit(solution)/shard_map/ppermute | solution.py:25
  371.3 4.2 %collective-permute-done.76 = f32[1,2048]{1,0:T(1,128)S(1)} collective-permute-done((f32[1,2048]{1,0:T(1,128)S(1)}, f32[1,2048]{1,0:T(1,128)S(1)}, u32[]{:S(2)}, u32[]{:S(2)}) %collective-permute-start.76) | collective-permute-done | bytes 8224 | tf_op jit(solution)/shard_map/ppermute | solution.py:26
  376.9 4.5 %collective-permute-start.79 = (f32[18,1]{1,0:T(8,128)S(1)}, f32[18,1]{1,0:T(8,128)S(1)}, u32[]{:S(2)}, u32[]{:S(2)}) collective-permute-start(f32[18,1]{1,0:T(8,128)S(1)} %get-tuple-element.60), channel_id=1, source_target_pairs={{0,1},{1,2},{2,3},{4,5},{5,6},{6,7},{8,9},{9,10},{10,11},{12,13},{... | collective-permute-start | bytes 224 | tf_op jit(solution)/shard_map/ppermute | solution.py:25
  (283 shorter events, 126.1 us)
Async XLA Ops:
  1.1 82.6 %collective-permute-start.1 = (f32[1,2048]{1,0:T(1,128)S(1)}, f32[1,2048]{1,0:T(1,128)S(1)}, u32[]{:S(2)}, u32[]{:S(2)}) collective-permute-start(f32[1,2048]{1,0:T(1,128)S(1)} %get-tuple-element.75), channel_id=1, source_target_pairs={{4,0},{8,4},{12,8},{5,1},{9,5},{13,9},{6,2},{10,6},{14,10},{7,3},{... | collective-permute-start | bytes 24584 | tf_op jit(solution)/shard_map/ppermute | solution.py:26
  2.4 81.3 %collective-permute-start = (f32[1,2048]{1,0:T(1,128)S(1)}, f32[1,2048]{1,0:T(1,128)S(1)}, u32[]{:S(2)}, u32[]{:S(2)}) collective-permute-start(f32[1,2048]{1,0:T(1,128)S(1)} %get-tuple-element.76), channel_id=1, source_target_pairs={{0,4},{4,8},{8,12},{1,5},{5,9},{9,13},{2,6},{6,10},{10,14},{3,7},{... | collective-permute-start | bytes 24584 | tf_op jit(solution)/shard_map/ppermute | solution.py:25
  23.1 56.0 %collective-permute-start.13 = (f32[1,1024]{1,0:T(1,128)S(1)}, f32[1,1024]{1,0:T(1,128)S(1)}, u32[]{:S(2)}, u32[]{:S(2)}) collective-permute-start(f32[1,1024]{1,0:T(1,128)S(1)} %get-tuple-element.95), channel_id=1, source_target_pairs={{4,0},{8,4},{12,8},{5,1},{9,5},{13,9},{6,2},{10,6},{14,10},{7,3},{... | collective-permute-start | bytes 12296 | tf_op jit(solution)/shard_map/ppermute | solution.py:26
  27.5 48.3 %collective-permute-start.37 = (f32[1,256]{1,0:T(1,128)S(1)}, f32[1,256]{1,0:T(1,128)S(1)}, u32[]{:S(2)}, u32[]{:S(2)}) collective-permute-start(f32[1,256]{1,0:T(1,128)S(1)} %get-tuple-element.141), channel_id=1, source_target_pairs={{4,0},{8,4},{12,8},{5,1},{9,5},{13,9},{6,2},{10,6},{14,10},{7,3},{... | collective-permute-start | bytes 3080 | tf_op jit(solution)/shard_map/ppermute | solution.py:26
  28.8 48.3 %collective-permute-start.36 = (f32[1,256]{1,0:T(1,128)S(1)}, f32[1,256]{1,0:T(1,128)S(1)}, u32[]{:S(2)}, u32[]{:S(2)}) collective-permute-start(f32[1,256]{1,0:T(1,128)S(1)} %get-tuple-element.142), channel_id=1, source_target_pairs={{0,4},{4,8},{8,12},{1,5},{5,9},{9,13},{2,6},{6,10},{10,14},{3,7},{... | collective-permute-start | bytes 3080 | tf_op jit(solution)/shard_map/ppermute | solution.py:25
  75.9 7.8 %collective-permute-start.12 = (f32[1,1024]{1,0:T(1,128)S(1)}, f32[1,1024]{1,0:T(1,128)S(1)}, u32[]{:S(2)}, u32[]{:S(2)}) collective-permute-start(f32[1,1024]{1,0:T(1,128)S(1)} %get-tuple-element.96), channel_id=1, source_target_pairs={{0,4},{4,8},{8,12},{1,5},{5,9},{9,13},{2,6},{6,10},{10,14},{3,7},{... | collective-permute-start | bytes 12296 | tf_op jit(solution)/shard_map/ppermute | solution.py:25
  77.2 65.8 %collective-permute-start.25 = (f32[1,512]{1,0:T(1,128)S(1)}, f32[1,512]{1,0:T(1,128)S(1)}, u32[]{:S(2)}, u32[]{:S(2)}) collective-permute-start(f32[1,512]{1,0:T(1,128)S(1)} %get-tuple-element.119), channel_id=1, source_target_pairs={{4,0},{8,4},{12,8},{5,1},{9,5},{13,9},{6,2},{10,6},{14,10},{7,3},{... | collective-permute-start | bytes 6152 | tf_op jit(solution)/shard_map/ppermute | solution.py:26
  79.1 63.9 %collective-permute-start.24 = (f32[1,512]{1,0:T(1,128)S(1)}, f32[1,512]{1,0:T(1,128)S(1)}, u32[]{:S(2)}, u32[]{:S(2)}) collective-permute-start(f32[1,512]{1,0:T(1,128)S(1)} %get-tuple-element.120), channel_id=1, source_target_pairs={{0,4},{4,8},{8,12},{1,5},{5,9},{9,13},{2,6},{6,10},{10,14},{3,7},{... | collective-permute-start | bytes 6152 | tf_op jit(solution)/shard_map/ppermute | solution.py:25
  90.4 12.9 %collective-permute-start.5 = (f32[1,2048]{1,0:T(1,128)S(1)}, f32[1,2048]{1,0:T(1,128)S(1)}, u32[]{:S(2)}, u32[]{:S(2)}) collective-permute-start(f32[1,2048]{1,0:T(1,128)S(1)} %get-tuple-element.73), channel_id=1, source_target_pairs={{0,4},{4,8},{8,12},{1,5},{5,9},{9,13},{2,6},{6,10},{10,14},{3,7},{... | collective-permute-start | bytes 24584 | tf_op jit(solution)/shard_map/ppermute | solution.py:25
  92.3 11.0 %collective-permute-start.4 = (f32[1,2048]{1,0:T(1,128)S(1)}, f32[1,2048]{1,0:T(1,128)S(1)}, u32[]{:S(2)}, u32[]{:S(2)}) collective-permute-start(f32[1,2048]{1,0:T(1,128)S(1)} %get-tuple-element.74), channel_id=1, source_target_pairs={{4,0},{8,4},{12,8},{5,1},{9,5},{13,9},{6,2},{10,6},{14,10},{7,3},{... | collective-permute-start | bytes 24584 | tf_op jit(solution)/shard_map/ppermute | solution.py:26
  97.3 5.9 %collective-permute-start.14 = (f32[10,1]{1,0:T(8,128)S(1)}, f32[10,1]{1,0:T(8,128)S(1)}, u32[]{:S(2)}, u32[]{:S(2)}) collective-permute-start(f32[10,1]{1,0:T(8,128)S(1)} %get-tuple-element.78), channel_id=1, source_target_pairs={{0,1},{1,2},{2,3},{4,5},{5,6},{6,7},{8,9},{9,10},{10,11},{12,13},{... | collective-permute-start | bytes 128 | tf_op jit(solution)/shard_map/ppermute | solution.py:25
  108.8 5.9 %collective-permute-start.9 = (f32[1,2048]{1,0:T(1,128)S(1)}, f32[1,2048]{1,0:T(1,128)S(1)}, u32[]{:S(2)}, u32[]{:S(2)}) collective-permute-start(f32[1,2048]{1,0:T(1,128)S(1)} %get-tuple-element.71), channel_id=1, source_target_pairs={{0,4},{4,8},{8,12},{1,5},{5,9},{9,13},{2,6},{6,10},{10,14},{3,7},{... | collective-permute-start | bytes 24584 | tf_op jit(solution)/shard_map/ppermute | solution.py:25
  113.3 5.5 %collective-permute-start.8 = (f32[1,2048]{1,0:T(1,128)S(1)}, f32[1,2048]{1,0:T(1,128)S(1)}, u32[]{:S(2)}, u32[]{:S(2)}) collective-permute-start(f32[1,2048]{1,0:T(1,128)S(1)} %get-tuple-element.72), channel_id=1, source_target_pairs={{4,0},{8,4},{12,8},{5,1},{9,5},{13,9},{6,2},{10,6},{14,10},{7,3},{... | collective-permute-start | bytes 24584 | tf_op jit(solution)/shard_map/ppermute | solution.py:26
  139.6 10.1 %collective-permute-start.17 = (f32[1,1024]{1,0:T(1,128)S(1)}, f32[1,1024]{1,0:T(1,128)S(1)}, u32[]{:S(2)}, u32[]{:S(2)}) collective-permute-start(f32[1,1024]{1,0:T(1,128)S(1)} %get-tuple-element.93), channel_id=1, source_target_pairs={{0,4},{4,8},{8,12},{1,5},{5,9},{9,13},{2,6},{6,10},{10,14},{3,7},{... | collective-permute-start | bytes 12296 | tf_op jit(solution)/shard_map/ppermute | solution.py:25
  141.7 7.9 %collective-permute-start.16 = (f32[1,1024]{1,0:T(1,128)S(1)}, f32[1,1024]{1,0:T(1,128)S(1)}, u32[]{:S(2)}, u32[]{:S(2)}) collective-permute-start(f32[1,1024]{1,0:T(1,128)S(1)} %get-tuple-element.94), channel_id=1, source_target_pairs={{4,0},{8,4},{12,8},{5,1},{9,5},{13,9},{6,2},{10,6},{14,10},{7,3},{... | collective-permute-start | bytes 12296 | tf_op jit(solution)/shard_map/ppermute | solution.py:26
  143.1 20.4 %collective-permute-start.26 = (f32[6,1]{1,0:T(8,128)S(1)}, f32[6,1]{1,0:T(8,128)S(1)}, u32[]{:S(2)}, u32[]{:S(2)}) collective-permute-start(f32[6,1]{1,0:T(8,128)S(1)} %get-tuple-element.107), channel_id=1, source_target_pairs={{0,1},{1,2},{2,3},{4,5},{5,6},{6,7},{8,9},{9,10},{10,11},{12,13},{... | collective-permute-start | bytes 80 | tf_op jit(solution)/shard_map/ppermute | solution.py:25
  148.3 15.2 %collective-permute-start.27 = (f32[6,1]{1,0:T(8,128)S(1)}, f32[6,1]{1,0:T(8,128)S(1)}, u32[]{:S(2)}, u32[]{:S(2)}) collective-permute-start(f32[6,1]{1,0:T(8,128)S(1)} %get-tuple-element.108), channel_id=1, source_target_pairs={{1,0},{2,1},{3,2},{5,4},{6,5},{7,6},{9,8},{10,9},{11,10},{13,12},{... | collective-permute-start | bytes 80 | tf_op jit(solution)/shard_map/ppermute | solution.py:26
  149.7 7.0 %collective-permute-start.18 = (f32[10,1]{1,0:T(8,128)S(1)}, f32[10,1]{1,0:T(8,128)S(1)}, u32[]{:S(2)}, u32[]{:S(2)}) collective-permute-start(f32[10,1]{1,0:T(8,128)S(1)} %get-tuple-element.85), channel_id=1, source_target_pairs={{1,0},{2,1},{3,2},{5,4},{6,5},{7,6},{9,8},{10,9},{11,10},{13,12},{... | collective-permute-start | bytes 128 | tf_op jit(solution)/shard_map/ppermute | solution.py:26
  151.0 6.6 %collective-permute-start.19 = (f32[10,1]{1,0:T(8,128)S(1)}, f32[10,1]{1,0:T(8,128)S(1)}, u32[]{:S(2)}, u32[]{:S(2)}) collective-permute-start(f32[10,1]{1,0:T(8,128)S(1)} %get-tuple-element.86), channel_id=1, source_target_pairs={{0,1},{1,2},{2,3},{4,5},{5,6},{6,7},{8,9},{9,10},{10,11},{12,13},{... | collective-permute-start | bytes 128 | tf_op jit(solution)/shard_map/ppermute | solution.py:25
  157.7 6.0 %collective-permute-start.21 = (f32[1,1024]{1,0:T(1,128)S(1)}, f32[1,1024]{1,0:T(1,128)S(1)}, u32[]{:S(2)}, u32[]{:S(2)}) collective-permute-start(f32[1,1024]{1,0:T(1,128)S(1)} %get-tuple-element.91), channel_id=1, source_target_pairs={{0,4},{4,8},{8,12},{1,5},{5,9},{9,13},{2,6},{6,10},{10,14},{3,7},{... | collective-permute-start | bytes 12296 | tf_op jit(solution)/shard_map/ppermute | solution.py:25
  162.2 5.5 %collective-permute-start.20 = (f32[1,1024]{1,0:T(1,128)S(1)}, f32[1,1024]{1,0:T(1,128)S(1)}, u32[]{:S(2)}, u32[]{:S(2)}) collective-permute-start(f32[1,1024]{1,0:T(1,128)S(1)} %get-tuple-element.92), channel_id=1, source_target_pairs={{4,0},{8,4},{12,8},{5,1},{9,5},{13,9},{6,2},{10,6},{14,10},{7,3},{... | collective-permute-start | bytes 12296 | tf_op jit(solution)/shard_map/ppermute | solution.py:26
  176.5 10.4 %collective-permute-start.29 = (f32[1,512]{1,0:T(1,128)S(1)}, f32[1,512]{1,0:T(1,128)S(1)}, u32[]{:S(2)}, u32[]{:S(2)}) collective-permute-start(f32[1,512]{1,0:T(1,128)S(1)} %get-tuple-element.117), channel_id=1, source_target_pairs={{0,4},{4,8},{8,12},{1,5},{5,9},{9,13},{2,6},{6,10},{10,14},{3,7},{... | collective-permute-start | bytes 6152 | tf_op jit(solution)/shard_map/ppermute | solution.py:25
  178.5 8.4 %collective-permute-start.28 = (f32[1,512]{1,0:T(1,128)S(1)}, f32[1,512]{1,0:T(1,128)S(1)}, u32[]{:S(2)}, u32[]{:S(2)}) collective-permute-start(f32[1,512]{1,0:T(1,128)S(1)} %get-tuple-element.118), channel_id=1, source_target_pairs={{4,0},{8,4},{12,8},{5,1},{9,5},{13,9},{6,2},{10,6},{14,10},{7,3},{... | collective-permute-start | bytes 6152 | tf_op jit(solution)/shard_map/ppermute | solution.py:26
  180.5 20.2 %collective-permute-start.38 = (f32[4,1]{1,0:T(4,128)S(1)}, f32[4,1]{1,0:T(4,128)S(1)}, u32[]{:S(2)}, u32[]{:S(2)}) collective-permute-start(f32[4,1]{1,0:T(4,128)S(1)} %get-tuple-element.129), channel_id=1, source_target_pairs={{0,1},{1,2},{2,3},{4,5},{5,6},{6,7},{8,9},{9,10},{10,11},{12,13},{... | collective-permute-start | bytes 56 | tf_op jit(solution)/shard_map/ppermute | solution.py:25
  185.5 15.2 %collective-permute-start.39 = (f32[4,1]{1,0:T(4,128)S(1)}, f32[4,1]{1,0:T(4,128)S(1)}, u32[]{:S(2)}, u32[]{:S(2)}) collective-permute-start(f32[4,1]{1,0:T(4,128)S(1)} %get-tuple-element.130), channel_id=1, source_target_pairs={{1,0},{2,1},{3,2},{5,4},{6,5},{7,6},{9,8},{10,9},{11,10},{13,12},{... | collective-permute-start | bytes 56 | tf_op jit(solution)/shard_map/ppermute | solution.py:26
  186.9 7.0 %collective-permute-start.30 = (f32[6,1]{1,0:T(8,128)S(1)}, f32[6,1]{1,0:T(8,128)S(1)}, u32[]{:S(2)}, u32[]{:S(2)}) collective-permute-start(f32[6,1]{1,0:T(8,128)S(1)} %get-tuple-element.105), channel_id=1, source_target_pairs={{1,0},{2,1},{3,2},{5,4},{6,5},{7,6},{9,8},{10,9},{11,10},{13,12},{... | collective-permute-start | bytes 80 | tf_op jit(solution)/shard_map/ppermute | solution.py:26
  188.2 6.5 %collective-permute-start.31 = (f32[6,1]{1,0:T(8,128)S(1)}, f32[6,1]{1,0:T(8,128)S(1)}, u32[]{:S(2)}, u32[]{:S(2)}) collective-permute-start(f32[6,1]{1,0:T(8,128)S(1)} %get-tuple-element.106), channel_id=1, source_target_pairs={{0,1},{1,2},{2,3},{4,5},{5,6},{6,7},{8,9},{9,10},{10,11},{12,13},{... | collective-permute-start | bytes 80 | tf_op jit(solution)/shard_map/ppermute | solution.py:25
  194.9 6.6 %collective-permute-start.33 = (f32[1,512]{1,0:T(1,128)S(1)}, f32[1,512]{1,0:T(1,128)S(1)}, u32[]{:S(2)}, u32[]{:S(2)}) collective-permute-start(f32[1,512]{1,0:T(1,128)S(1)} %get-tuple-element.115), channel_id=1, source_target_pairs={{0,4},{4,8},{8,12},{1,5},{5,9},{9,13},{2,6},{6,10},{10,14},{3,7},{... | collective-permute-start | bytes 6152 | tf_op jit(solution)/shard_map/ppermute | solution.py:25
  199.4 5.5 %collective-permute-start.32 = (f32[1,512]{1,0:T(1,128)S(1)}, f32[1,512]{1,0:T(1,128)S(1)}, u32[]{:S(2)}, u32[]{:S(2)}) collective-permute-start(f32[1,512]{1,0:T(1,128)S(1)} %get-tuple-element.116), channel_id=1, source_target_pairs={{4,0},{8,4},{12,8},{5,1},{9,5},{13,9},{6,2},{10,6},{14,10},{7,3},{... | collective-permute-start | bytes 6152 | tf_op jit(solution)/shard_map/ppermute | solution.py:26
  213.8 5.5 %collective-permute-start.40 = (f32[1,256]{1,0:T(1,128)S(1)}, f32[1,256]{1,0:T(1,128)S(1)}, u32[]{:S(2)}, u32[]{:S(2)}) collective-permute-start(f32[1,256]{1,0:T(1,128)S(1)} %get-tuple-element.140), channel_id=1, source_target_pairs={{4,0},{8,4},{12,8},{5,1},{9,5},{13,9},{6,2},{10,6},{14,10},{7,3},{... | collective-permute-start | bytes 3080 | tf_op jit(solution)/shard_map/ppermute | solution.py:26
  219.3 5.8 %collective-permute-start.42 = (f32[4,1]{1,0:T(4,128)S(1)}, f32[4,1]{1,0:T(4,128)S(1)}, u32[]{:S(2)}, u32[]{:S(2)}) collective-permute-start(f32[4,1]{1,0:T(4,128)S(1)} %get-tuple-element.127), channel_id=1, source_target_pairs={{1,0},{2,1},{3,2},{5,4},{6,5},{7,6},{9,8},{10,9},{11,10},{13,12},{... | collective-permute-start | bytes 56 | tf_op jit(solution)/shard_map/ppermute | solution.py:26
  229.0 5.5 %collective-permute-start.44 = (f32[1,256]{1,0:T(1,128)S(1)}, f32[1,256]{1,0:T(1,128)S(1)}, u32[]{:S(2)}, u32[]{:S(2)}) collective-permute-start(f32[1,256]{1,0:T(1,128)S(1)} %get-tuple-element.138), channel_id=1, source_target_pairs={{4,0},{8,4},{12,8},{5,1},{9,5},{13,9},{6,2},{10,6},{14,10},{7,3},{... | collective-permute-start | bytes 3080 | tf_op jit(solution)/shard_map/ppermute | solution.py:26
  234.5 5.7 %collective-permute-start.46 = (f32[4,1]{1,0:T(4,128)S(1)}, f32[4,1]{1,0:T(4,128)S(1)}, u32[]{:S(2)}, u32[]{:S(2)}) collective-permute-start(f32[4,1]{1,0:T(4,128)S(1)} %get-tuple-element.125), channel_id=1, source_target_pairs={{1,0},{2,1},{3,2},{5,4},{6,5},{7,6},{9,8},{10,9},{11,10},{13,12},{... | collective-permute-start | bytes 56 | tf_op jit(solution)/shard_map/ppermute | solution.py:26
  269.1 5.5 %collective-permute-start.48 = (f32[1,256]{1,0:T(1,128)S(1)}, f32[1,256]{1,0:T(1,128)S(1)}, u32[]{:S(2)}, u32[]{:S(2)}) collective-permute-start(f32[1,256]{1,0:T(1,128)S(1)} %get-tuple-element.134), channel_id=1, source_target_pairs={{4,0},{8,4},{12,8},{5,1},{9,5},{13,9},{6,2},{10,6},{14,10},{7,3},{... | collective-permute-start | bytes 3080 | tf_op jit(solution)/shard_map/ppermute | solution.py:26
  282.2 5.5 %collective-permute-start.52 = (f32[1,256]{1,0:T(1,128)S(1)}, f32[1,256]{1,0:T(1,128)S(1)}, u32[]{:S(2)}, u32[]{:S(2)}) collective-permute-start(f32[1,256]{1,0:T(1,128)S(1)} %get-tuple-element.132), channel_id=1, source_target_pairs={{4,0},{8,4},{12,8},{5,1},{9,5},{13,9},{6,2},{10,6},{14,10},{7,3},{... | collective-permute-start | bytes 3080 | tf_op jit(solution)/shard_map/ppermute | solution.py:26
  296.8 5.5 %collective-permute-start.56 = (f32[1,512]{1,0:T(1,128)S(1)}, f32[1,512]{1,0:T(1,128)S(1)}, u32[]{:S(2)}, u32[]{:S(2)}) collective-permute-start(f32[1,512]{1,0:T(1,128)S(1)} %get-tuple-element.112), channel_id=1, source_target_pairs={{4,0},{8,4},{12,8},{5,1},{9,5},{13,9},{6,2},{10,6},{14,10},{7,3},{... | collective-permute-start | bytes 6152 | tf_op jit(solution)/shard_map/ppermute | solution.py:26
  310.3 5.5 %collective-permute-start.60 = (f32[1,512]{1,0:T(1,128)S(1)}, f32[1,512]{1,0:T(1,128)S(1)}, u32[]{:S(2)}, u32[]{:S(2)}) collective-permute-start(f32[1,512]{1,0:T(1,128)S(1)} %get-tuple-element.110), channel_id=1, source_target_pairs={{4,0},{8,4},{12,8},{5,1},{9,5},{13,9},{6,2},{10,6},{14,10},{7,3},{... | collective-permute-start | bytes 6152 | tf_op jit(solution)/shard_map/ppermute | solution.py:26
  315.9 5.8 %collective-permute-start.62 = (f32[6,1]{1,0:T(8,128)S(1)}, f32[6,1]{1,0:T(8,128)S(1)}, u32[]{:S(2)}, u32[]{:S(2)}) collective-permute-start(f32[6,1]{1,0:T(8,128)S(1)} %get-tuple-element.99), channel_id=1, source_target_pairs={{1,0},{2,1},{3,2},{5,4},{6,5},{7,6},{9,8},{10,9},{11,10},{13,12},{... | collective-permute-start | bytes 80 | tf_op jit(solution)/shard_map/ppermute | solution.py:26
  325.3 5.5 %collective-permute-start.64 = (f32[1,1024]{1,0:T(1,128)S(1)}, f32[1,1024]{1,0:T(1,128)S(1)}, u32[]{:S(2)}, u32[]{:S(2)}) collective-permute-start(f32[1,1024]{1,0:T(1,128)S(1)} %get-tuple-element.90), channel_id=1, source_target_pairs={{4,0},{8,4},{12,8},{5,1},{9,5},{13,9},{6,2},{10,6},{14,10},{7,3},{... | collective-permute-start | bytes 12296 | tf_op jit(solution)/shard_map/ppermute | solution.py:26
  330.9 5.8 %collective-permute-start.66 = (f32[10,1]{1,0:T(8,128)S(1)}, f32[10,1]{1,0:T(8,128)S(1)}, u32[]{:S(2)}, u32[]{:S(2)}) collective-permute-start(f32[10,1]{1,0:T(8,128)S(1)} %get-tuple-element.81), channel_id=1, source_target_pairs={{1,0},{2,1},{3,2},{5,4},{6,5},{7,6},{9,8},{10,9},{11,10},{13,12},{... | collective-permute-start | bytes 128 | tf_op jit(solution)/shard_map/ppermute | solution.py:26
  339.8 5.5 %collective-permute-start.68 = (f32[1,1024]{1,0:T(1,128)S(1)}, f32[1,1024]{1,0:T(1,128)S(1)}, u32[]{:S(2)}, u32[]{:S(2)}) collective-permute-start(f32[1,1024]{1,0:T(1,128)S(1)} %get-tuple-element.88), channel_id=1, source_target_pairs={{4,0},{8,4},{12,8},{5,1},{9,5},{13,9},{6,2},{10,6},{14,10},{7,3},{... | collective-permute-start | bytes 12296 | tf_op jit(solution)/shard_map/ppermute | solution.py:26
  345.3 5.8 %collective-permute-start.70 = (f32[10,1]{1,0:T(8,128)S(1)}, f32[10,1]{1,0:T(8,128)S(1)}, u32[]{:S(2)}, u32[]{:S(2)}) collective-permute-start(f32[10,1]{1,0:T(8,128)S(1)} %get-tuple-element.79), channel_id=1, source_target_pairs={{1,0},{2,1},{3,2},{5,4},{6,5},{7,6},{9,8},{10,9},{11,10},{13,12},{... | collective-permute-start | bytes 128 | tf_op jit(solution)/shard_map/ppermute | solution.py:26
  355.3 5.5 %collective-permute-start.72 = (f32[1,2048]{1,0:T(1,128)S(1)}, f32[1,2048]{1,0:T(1,128)S(1)}, u32[]{:S(2)}, u32[]{:S(2)}) collective-permute-start(f32[1,2048]{1,0:T(1,128)S(1)} %get-tuple-element.70), channel_id=1, source_target_pairs={{4,0},{8,4},{12,8},{5,1},{9,5},{13,9},{6,2},{10,6},{14,10},{7,3},{... | collective-permute-start | bytes 24584 | tf_op jit(solution)/shard_map/ppermute | solution.py:26
  361.0 5.8 %collective-permute-start.74 = (f32[18,1]{1,0:T(8,128)S(1)}, f32[18,1]{1,0:T(8,128)S(1)}, u32[]{:S(2)}, u32[]{:S(2)}) collective-permute-start(f32[18,1]{1,0:T(8,128)S(1)} %get-tuple-element.61), channel_id=1, source_target_pairs={{1,0},{2,1},{3,2},{5,4},{6,5},{7,6},{9,8},{10,9},{11,10},{13,12},{... | collective-permute-start | bytes 224 | tf_op jit(solution)/shard_map/ppermute | solution.py:26
  362.2 5.3 %collective-permute-start.75 = (f32[18,1]{1,0:T(8,128)S(1)}, f32[18,1]{1,0:T(8,128)S(1)}, u32[]{:S(2)}, u32[]{:S(2)}) collective-permute-start(f32[18,1]{1,0:T(8,128)S(1)} %get-tuple-element.62), channel_id=1, source_target_pairs={{0,1},{1,2},{2,3},{4,5},{5,6},{6,7},{8,9},{9,10},{10,11},{12,13},{... | collective-permute-start | bytes 224 | tf_op jit(solution)/shard_map/ppermute | solution.py:25
  370.0 5.5 %collective-permute-start.76 = (f32[1,2048]{1,0:T(1,128)S(1)}, f32[1,2048]{1,0:T(1,128)S(1)}, u32[]{:S(2)}, u32[]{:S(2)}) collective-permute-start(f32[1,2048]{1,0:T(1,128)S(1)} %get-tuple-element.68), channel_id=1, source_target_pairs={{4,0},{8,4},{12,8},{5,1},{9,5},{13,9},{6,2},{10,6},{14,10},{7,3},{... | collective-permute-start | bytes 24584 | tf_op jit(solution)/shard_map/ppermute | solution.py:26
  375.6 5.8 %collective-permute-start.78 = (f32[18,1]{1,0:T(8,128)S(1)}, f32[18,1]{1,0:T(8,128)S(1)}, u32[]{:S(2)}, u32[]{:S(2)}) collective-permute-start(f32[18,1]{1,0:T(8,128)S(1)} %get-tuple-element.59), channel_id=1, source_target_pairs={{1,0},{2,1},{3,2},{5,4},{6,5},{7,6},{9,8},{10,9},{11,10},{13,12},{... | collective-permute-start | bytes 224 | tf_op jit(solution)/shard_map/ppermute | solution.py:26
  376.9 5.4 %collective-permute-start.79 = (f32[18,1]{1,0:T(8,128)S(1)}, f32[18,1]{1,0:T(8,128)S(1)}, u32[]{:S(2)}, u32[]{:S(2)}) collective-permute-start(f32[18,1]{1,0:T(8,128)S(1)} %get-tuple-element.60), channel_id=1, source_target_pairs={{0,1},{1,2},{2,3},{4,5},{5,6},{6,7},{8,9},{9,10},{10,11},{12,13},{... | collective-permute-start | bytes 224 | tf_op jit(solution)/shard_map/ppermute | solution.py:25
  (42 other events, 372.0 us)
where the time goes:
time: 389 us; the launch traced here: 383 us
  starting transfers between devices  191 us (49%)
  waiting for transfers between devices  69.3 us (18%)
  local copies, waits for them, and re-layouts  45.4 us (12%)
  blocking collectives  43.3 us (11%)
  other arithmetic  32.2 us (8%)
    ppermute x40, starting transfers between devices, extended(): before = lax.ppermute(last, axis, up)  140 us
    ppermute x40, waiting for transfers between devices, extended(): after = lax.ppermute(leading, axis, down)  54.7 us
    ppermute x40, starting transfers between devices, extended(): after = lax.ppermute(leading, axis, down)  51.5 us
    reshape x7, local copies, waits for them, and re-layouts, coarsen_sum(): field.reshape(field.shape[0] // 2, 2, field.shape[1] // 2, 2)  36.8 us
    all_gather x1, blocking collectives, body(): lax.all_gather(right_side[None, None], ('sub', 'blk'), axis=0, tiled=True)  22.8 us
    all_gather x1, blocking collectives, body(): coef_all = lax.all_gather(paired, ('sub', 'blk'), axis=0, tiled=True)  20.5 us
    reduce_sum x18, other arithmetic, coarsen_sum(): field.reshape(field.shape[0] // 2, 2, field.shape[1] // 2, 2)  18.3 us
    ppermute x40, waiting for transfers between devices, extended(): before = lax.ppermute(last, axis, up)  14.6 us
  transfers between devices with their start and end apart: 80, of which 32 were waited for; matrix products, arithmetic and copies ran while one was open for 16% of the time, Pallas kernels for 0%

commit v1 on v0

v1 whole, which is shorter than its diff:
```python
import functools
import jax
import jax.numpy as jnp
from jax import lax
from jax.experimental import pallas as pl
from jax.experimental.pallas import tpu as pltpu
from jax.sharding import PartitionSpec as P

LEVELS = 5
SMOOTH = (2, 0.5, 2.0)
COARSE_LOW, COARSE_HIGH = 0.02, 2.0
DIRS = ((-1, 0), (1, 0), (0, -1), (0, 1), (-1, -1), (-1, 1), (1, -1), (1, 1))
MESH = pl.DeviceIdType.MESH


def round_up(n, k):
    return -(-n // k) * k


def chebyshev_terms(sweep_count, low_end, high_end):
    mid = 0.5 * (high_end + low_end)
    half = 0.5 * (high_end - low_end)
    sigma = mid / half
    rho = 1.0 / sigma
    terms = [(0.0, 1.0 / mid)]
    for _ in range(1, sweep_count):
        rho_next = 1.0 / (2.0 * sigma - rho)
        terms.append((rho_next * rho, 2.0 * rho_next / half))
        rho = rho_next
    return terms


def rolled(x, shift, axis):
    return pltpu.roll(x, shift % x.shape[axis], axis)


def level_operator(c, g, whole_rows):
    rows, cols = c.shape
    h = 0.5 * c
    valid = c > 0.0
    c_r = rolled(c, -1, 1)
    c_d = rolled(c, -1, 0)
    e_r = jnp.where(valid & (c_r > 0.0), h + 0.5 * c_r, 0.0)
    ok_d = valid & (c_d > 0.0)
    if whole_rows:
        ok_d = ok_d & (lax.broadcasted_iota(jnp.int32, c.shape, 0) < rows - 1)
    e_d = jnp.where(ok_d, h + 0.5 * c_d, 0.0)
    e_l = rolled(e_r, 1, 1)
    e_u = rolled(e_d, 1, 0)
    m = jnp.where(valid, 1.0, 0.0)
    diag = e_d + e_u + e_r + e_l + g + (1.0 - m)
    inv = 1.0 / jnp.maximum(diag, 0.25 * c)
    return e_r, e_l, e_d, e_u, diag, inv, m


def residual(op, f, x):
    e_r, e_l, e_d, e_u, diag, inv, m = op
    out = f - diag * x
    out = out + e_r * rolled(x, -1, 1) + e_l * rolled(x, 1, 1)
    return out + e_d * rolled(x, -1, 0) + e_u * rolled(x, 1, 0)


def smooth(op, f, x, terms):
    d = None
    for keep, fresh in terms:
        r = f if x is None else residual(op, f, x)
        step = fresh * (r * op[5])
        d = step if d is None else keep * d + step
        x = d if x is None else x + d
    return x


def split_dot(x, w):
    hi = x.astype(jnp.bfloat16)
    lo = (x - hi.astype(jnp.float32)).astype(jnp.bfloat16)
    return jnp.dot(hi, w, preferred_element_type=jnp.float32) + jnp.dot(
        lo, w, preferred_element_type=jnp.float32
    )


def coarsen(x, tmp, pair):
    rows, cols = x.shape
    if cols % 256:
        x = jnp.concatenate([x, jnp.zeros((rows, 128), jnp.float32)], axis=1)
        cols += 128
    k = cols // 256
    stack = jnp.concatenate([x[:, 256 * j : 256 * j + 256] for j in range(k)], axis=0)
    tmp[: rows * k, :] = split_dot(stack, pair)
    n = rows * k // 2
    s = tmp[pl.ds(0, n, stride=2), :] + tmp[pl.ds(1, n, stride=2), :]
    half = rows // 2
    return [s[half * j : half * (j + 1)] for j in range(k)]


def prolong(x, tmp, pair_t, cols):
    rows = x.shape[0]
    k = x.shape[1] // 128
    for j in range(k):
        tile = x[:, 128 * j : 128 * j + 128]
        tmp[pl.ds(2 * rows * j, rows, stride=2), :] = tile
        tmp[pl.ds(2 * rows * j + 1, rows, stride=2), :] = tile
    out = split_dot(tmp[: 2 * rows * k, :], pair_t)
    out = [out[2 * rows * j : 2 * rows * (j + 1)] for j in range(k)]
    return jnp.concatenate(out, axis=1)[:, :cols]


def kernel(
    plan,
    cond, src, gnd, nod, out,
    c0, g0, f0, x0, c1, g1, f1, x1, c2, g2, f2, y2, f3, f4, tmp, tmp_up,
    a_row_s, a_row_r, a_col_s, a_col_r, a_cor_s, a_cor_r, a_sem,
    x0_s, x0_r, cg1_s, cg1_r, f1_s, f1_r, x1_s, x1_r, row_sem,
    cg2_g, f2_g, gather_sem,
):
    n_sub, n_blk, halo, widths, coarse_count = plan
    s, b = lax.axis_index("sub"), lax.axis_index("blk")
    w0, w1, w2, w3, w4 = widths
    own = out.shape[1]

    def exists(dr, dc):
        ok = None
        for need, cond_ in (
            (dr < 0, s > 0), (dr > 0, s < n_sub - 1), (dc < 0, b > 0), (dc > 0, b < n_blk - 1),
        ):
            if need:
                ok = cond_ if ok is None else ok & cond_
        return ok

    for ref in (c0, g0, f0, c1, g1, f1, y2, f3, f4):
        ref[...] = jnp.zeros_like(ref)

    barrier = pltpu.get_barrier_semaphore()
    for dr in range(n_sub):
        @pl.when(s != dr)
        def _():
            pl.semaphore_signal(barrier, 1, device_id={"sub": dr}, device_id_type=MESH)
    for dr, dc in DIRS[2:]:
        @pl.when(exists(dr, dc))
        def _():
            pl.semaphore_signal(
                barrier, 1, device_id={"sub": s + dr, "blk": b + dc}, device_id_type=MESH
            )

    valid = 1.0 - nod[...].astype(jnp.float32)
    c = cond[...] * valid
    g = gnd[...].astype(jnp.float32) * c
    f = valid * (src[...].astype(jnp.float32) - 0.125)
    c0[4:20, halo : halo + own] = c
    g0[4:20, halo : halo + own] = g
    f0[4:20, halo : halo + own] = f
    for i, (rc, rg) in enumerate(((slice(0, 3), slice(0, 2)), (slice(13, 16), slice(14, 16)))):
        a_row_s[i, 0:3] = c[rc]
        a_row_s[i, 3:5] = g[rg]
        a_row_s[i, 5:7] = f[rg]
        a_row_s[i, 7:8] = jnp.zeros((1, own), jnp.float32)
        for j, lanes in enumerate((slice(0, halo), slice(own - halo, own))):
            a_cor_s[2 * i + j, 0:3] = c[rc, lanes]
            a_cor_s[2 * i + j, 3:5] = g[rg, lanes]
            a_cor_s[2 * i + j, 5:7] = f[rg, lanes]
            a_cor_s[2 * i + j, 7:8] = jnp.zeros((1, halo), jnp.float32)
    for j, lanes in enumerate((slice(0, halo), slice(own - halo, own))):
        a_col_s[j, 0:16] = c[:, lanes]
        a_col_s[j, 16:32] = g[:, lanes]
        a_col_s[j, 32:48] = f[:, lanes]

    has = lambda flag: jnp.where(flag, 1, 0)
    partners = n_sub - 1
    for dr, dc in DIRS[2:]:
        partners = partners + has(exists(dr, dc))
    pl.semaphore_wait(barrier, partners)

    def remote(src_ref, dst_ref, send, recv, dr, dc=0):
        return pltpu.make_async_remote_copy(
            src_ref=src_ref, dst_ref=dst_ref, send_sem=send, recv_sem=recv,
            device_id={"sub": s + dr, "blk": b + dc}, device_id_type=MESH,
        )

    def a_copy(d):
        dr, dc = DIRS[d]
        if d < 2:
            pair_ = a_row_s.at[d], a_row_r.at[d]
        elif d < 4:
            pair_ = a_col_s.at[d - 2], a_col_r.at[d - 2]
        else:
            pair_ = a_cor_s.at[d - 4], a_cor_r.at[d - 4]
        return remote(*pair_, a_sem.at[0, d], a_sem.at[1, d], dr, dc)

    row_bufs = ((x0_s, x0_r), (cg1_s, cg1_r), (f1_s, f1_r), (x1_s, x1_r))

    def row_copy(e, d):
        send, recv = row_bufs[e]
        return remote(send.at[d], recv.at[d], row_sem.at[0, e, d], row_sem.at[1, e, d], DIRS[d][0])

    def row_start(e):
        for d in range(2):
            @pl.when(exists(*DIRS[d]))
            def _():
                row_copy(e, d).start()

    def row_wait(e, put):
        for d in range(2):
            @pl.when(exists(-DIRS[d][0], 0))
            def _():
                row_copy(e, d).wait_recv()
                put(d)

    def gather_copy(e, other, sender):
        buf = (cg2_g, f2_g)[e]
        return pltpu.make_async_remote_copy(
            src_ref=buf.at[sender], dst_ref=buf.at[sender],
            send_sem=gather_sem.at[0, e, other], recv_sem=gather_sem.at[1, e, sender],
            device_id={"sub": other}, device_id_type=MESH,
        )

    def gather_start(e):
        for other in range(n_sub):
            @pl.when(s != other)
            def _():
                gather_copy(e, other, s).start()

    def gather_wait(e):
        for other in range(n_sub):
            @pl.when(s != other)
            def _():
                gather_copy(e, other, other).wait_recv()

    for d in range(8):
        @pl.when(exists(*DIRS[d]))
        def _():
            a_copy(d).start()

    iota = lambda shape, dim: lax.broadcasted_iota(jnp.int32, shape, dim)
    pair = jnp.where(
        jnp.right_shift(iota((256, 128), 0), 1) == iota((256, 128), 1), 1.0, 0.0
    ).astype(jnp.bfloat16)
    pair_t = jnp.where(
        jnp.right_shift(iota((128, 256), 1), 1) == iota((128, 256), 0), 1.0, 0.0
    ).astype(jnp.bfloat16)

    for d, (dr, dc) in enumerate(DIRS):
        @pl.when(exists(-dr, -dc))
        def _():
            a_copy(d).wait_recv()
            lanes = {0: slice(halo, halo + own), 1: slice(0, halo), -1: slice(halo + own, w0)}[dc]
            if dr == 0:
                for k, ref in enumerate((c0, g0, f0)):
                    ref[4:20, lanes] = a_col_r[d - 2, 16 * k : 16 * k + 16]
            else:
                got = (a_row_r, d) if d < 2 else (a_cor_r, d - 4)
                got = got[0].at[got[1]]
                c0[slice(1, 4) if dr > 0 else slice(20, 23), lanes] = got[0:3]
                near = slice(2, 4) if dr > 0 else slice(20, 22)
                g0[near, lanes] = got[3:5]
                f0[near, lanes] = got[5:7]

    both = jnp.concatenate([0.25 * c0[4:20, :], g0[4:20, :]], axis=0)
    both = jnp.concatenate(coarsen(both, tmp, pair), axis=1)
    c1[4:12, :] = both[0:8]
    g1[4:12, :] = both[8:16]
    for i, (rc, rg) in enumerate(((slice(0, 3), slice(8, 10)), (slice(5, 8), slice(14, 16)))):
        cg1_s[i, 0:3] = both[rc]
        cg1_s[i, 3:5] = both[rg]
        cg1_s[i, 5:8] = jnp.zeros((3, w1), jnp.float32)
    row_start(1)
    both = jnp.concatenate([0.25 * both[0:8], both[8:16]], axis=0)
    both = jnp.concatenate(coarsen(both, tmp, pair), axis=1)
    cg2_g[s] = both
    gather_start(0)

    terms = chebyshev_terms(*SMOOTH)
    op0 = level_operator(c0[...], g0[...], False)
    f = f0[...]
    x = smooth(op0, f, None, terms)
    r = residual(op0, f, x)
    rhs = jnp.concatenate(coarsen(r[4:20], tmp, pair), axis=1)
    f1[4:12, :] = rhs
    f1_s[0] = rhs[0:2]
    f1_s[1] = rhs[6:8]
    row_start(2)
    x0[...] = x
    x0_s[0] = x[4:6]
    x0_s[1] = x[18:20]
    row_start(0)

    def put_cg1(d):
        c1[slice(12, 15) if d == 0 else slice(1, 4), :] = cg1_r[d, 0:3]
        g1[slice(12, 14) if d == 0 else slice(2, 4), :] = cg1_r[d, 3:5]

    row_wait(1, put_cg1)
    op1 = level_operator(c1[...], g1[...], False)

    def put_f1(d):
        f1[slice(12, 14) if d == 0 else slice(2, 4), :] = f1_r[d]

    row_wait(2, put_f1)
    fl1 = f1[...]
    x = smooth(op1, fl1, None, terms)
    r = residual(op1, fl1, x)
    f2_g[s] = jnp.concatenate(coarsen(r[4:12], tmp, pair), axis=1)
    gather_start(1)
    x1[...] = x
    x1_s[0] = x[4:7]
    x1_s[1] = x[9:12]
    row_start(3)

    gather_wait(0)
    for k in range(n_sub):
        c2[4 * k : 4 * k + 4, :] = cg2_g[k, 0:4]
        g2[4 * k : 4 * k + 4, :] = cg2_g[k, 4:8]

    cg = (c2[...], g2[...])
    ops = [level_operator(*cg, True)]
    rows = 4 * n_sub
    for level, width in ((3, w3), (4, w4)):
        rows //= 2
        full = max(rows, 8)
        parts = []
        for k, v in enumerate(cg):
            tiles = coarsen(0.25 * v if k == 0 else v, tmp, pair)
            v = jnp.concatenate(tiles, axis=1)[:rows]
            if full > rows:
                v = jnp.concatenate([v, jnp.zeros((full - rows, width), jnp.float32)], axis=0)
            parts.append(v)
        cg = tuple(parts)
        ops.append(level_operator(*cg, True))

    gather_wait(1)
    for k in range(n_sub):
        f2[4 * k : 4 * k + 4, :] = f2_g[k]
    rhs = f2[...]
    kept = []
    rows = 4 * n_sub
    for level in (2, 3):
        op = ops[level - 2]
        x = smooth(op, rhs, None, terms)
        r = residual(op, rhs, x)
        kept.append((rhs, x))
        rows //= 2
        ref = (f3, f4)[level - 2]
        for j, tile in enumerate(coarsen(r, tmp, pair)):
            ref[:rows, 128 * j : 128 * j + 128] = tile
        rhs = ref[...]
    y = smooth(ops[2], rhs, None, chebyshev_terms(coarse_count, COARSE_LOW, COARSE_HIGH))
    for level, width in ((3, w3), (2, w2)):
        op = ops[level - 2]
        rhs, x = kept[level - 2]
        rows = n_sub if level == 3 else 2 * n_sub
        y = x + op[6] * prolong(y[:rows], tmp_up, pair_t, width)
        y = smooth(op, rhs, y, terms)

    for k in range(n_sub):
        y2[k + 1] = y[4 * k : 4 * k + 4]
    y = jnp.concatenate([y2[s][2:4], y2[s + 1], y2[s + 2][0:2]], axis=0)

    def put_x1(d):
        x1[slice(12, 15) if d == 0 else slice(1, 4), :] = x1_r[d]

    row_wait(3, put_x1)
    y = x1[...] + op1[6] * prolong(y, tmp_up, pair_t, w1)
    y = smooth(op1, fl1, y, terms)

    def put_x0(d):
        x0[slice(20, 22) if d == 0 else slice(2, 4), :] = x0_r[d]

    row_wait(0, put_x0)
    y = x0[...] + op0[6] * prolong(y[2:14], tmp_up, pair_t, w0)
    y = smooth(op0, f0[...], y, terms)
    out[...] = y[4:20, halo : halo + own]

    for d in range(8):
        @pl.when(exists(*DIRS[d]))
        def _():
            a_copy(d).wait_send()
    for e in range(4):
        for d in range(2):
            @pl.when(exists(*DIRS[d]))
            def _():
                row_copy(e, d).wait_send()
    for e in range(2):
        for other in range(n_sub):
            @pl.when(s != other)
            def _():
                gather_copy(e, other, s).wait_send()


def body(conductance, source_mask, ground_mask, nodata_mask):
    n_sub, n_blk = lax.axis_size("sub"), lax.axis_size("blk")
    rows, own = conductance.shape
    assert rows == 16 and own % 256 == 0
    coarse_count = 8 + n_sub // 2
    need = coarse_count + 2
    for _ in range(LEVELS - 1):
        need = 2 * need + 2
    halo = round_up(need, 256)
    assert halo <= own
    w0 = own + 2 * halo
    widths = (w0,) + tuple(round_up(w0 >> l, 128) for l in range(1, 5))
    w1, w2, w3, w4 = widths[1:]
    f32 = lambda *shape: pltpu.VMEM(shape, jnp.float32)
    sem = lambda *shape: pltpu.SemaphoreType.DMA(shape)
    r2, r3, r4 = 4 * n_sub, max(2 * n_sub, 8), max(n_sub, 8)
    tmp_rows = max(32 * round_up(w0, 256) // 256, 4 * n_sub * round_up(w2, 256) // 256)
    up_rows = max(24 * w1 // 128, 4 * n_sub * w3 // 128)
    vmem = pl.BlockSpec(memory_space=pltpu.VMEM)
    return pl.pallas_call(
        functools.partial(kernel, (n_sub, n_blk, halo, widths, coarse_count)),
        out_shape=jax.ShapeDtypeStruct((rows, own), jnp.float32),
        in_specs=[vmem] * 4,
        out_specs=vmem,
        scratch_shapes=[
            f32(24, w0), f32(24, w0), f32(24, w0), f32(24, w0),
            f32(16, w1), f32(16, w1), f32(16, w1), f32(16, w1),
            f32(r2, w2), f32(r2, w2), f32(r2, w2), f32(n_sub + 2, 4, w2),
            f32(r3, w3), f32(r4, w4), f32(tmp_rows, 128), f32(up_rows, 128),
            f32(2, 8, own), f32(2, 8, own), f32(2, 48, halo), f32(2, 48, halo),
            f32(4, 8, halo), f32(4, 8, halo), sem(2, 8),
            f32(2, 2, w0), f32(2, 2, w0), f32(2, 8, w1), f32(2, 8, w1),
            f32(2, 2, w1), f32(2, 2, w1), f32(2, 3, w1), f32(2, 3, w1), sem(2, 4, 2),
            f32(n_sub, 8, w2), f32(n_sub, 4, w2), sem(2, 2, n_sub),
        ],
        compiler_params=pltpu.CompilerParams(
            collective_id=0, has_side_effects=True, vmem_limit_bytes=40 * 1024 * 1024
        ),
    )(conductance, source_mask, ground_mask, nodata_mask)


def solution(mesh):
    spec = P(("groups", "sub"), "blk")
    return jax.shard_map(
        body, mesh=mesh, in_specs=(spec,) * 4, out_specs=spec, check_vma=False
    )
```

time: 389 us -> 25.4 us (0.07); the launches traced: 383 us -> 25.2 us
  starting transfers between devices: 191 us -> 0 us
  waiting for transfers between devices: 69.3 us -> 0 us
  blocking collectives: 43.3 us -> 0 us
  local copies, waits for them, and re-layouts: 45.4 us -> 4.27 us
  other arithmetic: 32.2 us -> 0 us
  Pallas kernels: 0 us -> 20.9 us
    ppermute x80 -> x0, starting transfers between devices: 191 us -> none  [the longest x40 140 us: extended(): before = lax.ppermute(last, axis, up)]
    ppermute x80 -> x0, waiting for transfers between devices: 69.3 us -> none  [the longest x40 54.7 us: extended(): after = lax.ppermute(leading, axis, down)]
    all_gather x2 -> x0, blocking collectives: 43.3 us -> none  [the longest x1 22.8 us: body(): lax.all_gather(right_side[None, None], ('sub', 'blk'), axis=0, tiled=True)]
    reshape x17 -> x0, local copies, waits for them, and re-layouts: 37.9 us -> none  [the longest x7 36.8 us: coarsen_sum(): field.reshape(field.shape[0] // 2, 2, field.shape[1] // 2, 2)]
    pallas_call x0 -> x1, Pallas kernels: none -> 20.9 us  [body(): pl.pallas_call(functools.partial(kernel, (n_sub, n_blk, halo, widths, coa...]
    reduce_sum x18 -> x0, other arithmetic: 18.3 us -> none  [coarsen_sum(): field.reshape(field.shape[0] // 2, 2, field.shape[1] // 2, 2)]
    add x24 -> x0, other arithmetic: 5.79 us -> none  [the longest x20 5.03 us: smooth(): iterate = iterate + update]
  transfers between devices with their start and end apart: 80 -> 0, of which waited for: 32 -> 0; matrix products, arithmetic and copies ran while one was open for 16% -> 0% of each run, Pallas kernels for 0% -> 0%
where the time goes in v1:
time: 25.4 us; the launch traced here: 25.2 us
  Pallas kernels  20.9 us (82%)
  local copies, waits for them, and re-layouts  4.27 us (17%)
    pallas_call x1, Pallas kernels, body(): pl.pallas_call(functools.partial(kernel, (n_sub, n_blk, halo, widths, coa...  20.9 us
    unnamed x9, local copies, waits for them, and re-layouts  4.27 us

profile of v1, /device:TPU:0, one launch (start us, length us, event | category | flops | bytes accessed | tf_op | source)
XLA Modules:
  0.0 25.2 jit_solution(4311799605845410307)
XLA Ops:
  0.0 0.0 copy-start
  0.0 0.9 %copy-done = f32[16,2048]{1,0:T(8,128)S(1)} copy-done((f32[16,2048]{1,0:T(8,128)S(1)}, f32[16,2048]{1,0:T(8,128)}, u32[]{:S(2)}) %copy-start) | copy-done | bytes 131096
  0.9 0.0 copy-start.1
  0.9 0.9 %copy-done.1 = s32[16,2048]{1,0:T(8,128)S(1)} copy-done((s32[16,2048]{1,0:T(8,128)S(1)}, s32[16,2048]{1,0:T(8,128)}, u32[]{:S(2)}) %copy-start.1) | copy-done | bytes 131096
  1.8 0.0 copy-start.2
  1.8 0.9 %copy-done.2 = s32[16,2048]{1,0:T(8,128)S(1)} copy-done((s32[16,2048]{1,0:T(8,128)S(1)}, s32[16,2048]{1,0:T(8,128)}, u32[]{:S(2)}) %copy-start.2) | copy-done | bytes 131096
  2.7 0.0 copy-start.3
  2.7 0.9 %copy-done.3 = s32[16,2048]{1,0:T(8,128)S(1)} copy-done((s32[16,2048]{1,0:T(8,128)S(1)}, s32[16,2048]{1,0:T(8,128)}, u32[]{:S(2)}) %copy-start.3) | copy-done | bytes 131096
  3.6 20.9 %shard_map.46 = f32[16,2048]{1,0:T(8,128)S(1)} custom-call(f32[16,2048]{1,0:T(8,128)S(1)} %copy-done, s32[16,2048]{1,0:T(8,128)S(1)} %copy-done.1, s32[16,2048]{1,0:T(8,128)S(1)} %copy-done.2, s32[16,2048]{1,0:T(8,128)S(1)} %copy-done.3), custom_call_target="tpu_custom_call" | custom-call | tf_op jit(solution)/shard_map/pallas_call | solution.py:405
  24.5 0.7 %copy.6 = f32[16,2048]{1,0:T(8,128)} copy(f32[16,2048]{1,0:T(8,128)S(1)} %shard_map.46) | data formatting | bytes 262144
Async XLA Ops:
  0.0 0.9 %copy-start = (f32[16,2048]{1,0:T(8,128)S(1)}, f32[16,2048]{1,0:T(8,128)}, u32[]{:S(2)}) copy-start(f32[16,2048]{1,0:T(8,128)} %cond.1) | copy-start | bytes 393220
  0.9 0.9 %copy-start.1 = (s32[16,2048]{1,0:T(8,128)S(1)}, s32[16,2048]{1,0:T(8,128)}, u32[]{:S(2)}) copy-start(s32[16,2048]{1,0:T(8,128)} %src.1) | copy-start | bytes 393220
  1.8 0.9 %copy-start.2 = (s32[16,2048]{1,0:T(8,128)S(1)}, s32[16,2048]{1,0:T(8,128)}, u32[]{:S(2)}) copy-start(s32[16,2048]{1,0:T(8,128)} %gnd.1) | copy-start | bytes 393220
  2.7 0.9 %copy-start.3 = (s32[16,2048]{1,0:T(8,128)S(1)}, s32[16,2048]{1,0:T(8,128)}, u32[]{:S(2)}) copy-start(s32[16,2048]{1,0:T(8,128)} %nod.1) | copy-start | bytes 393220
